TPU v7x, 512 devices: a whole 4x4x16 slice. The times are simulated.
512 devices in a mesh: head: 8 (over x, core), tok: 64 (over z, y).
Axes of the slice: x: 4, y: 4, z: 16, core: 2. Of those that a mesh axis runs over, the one named last changes fastest.
Arguments:
- query_one: bfloat16 [16384, 4096], P(('head', 'tok')), may hold values from -6 to 6
- key_one: bfloat16 [16384, 4096], P(('head', 'tok')), may hold values from -6 to 6
- value_one: bfloat16 [16384, 4096], P(('head', 'tok')), may hold values from -6 to 6
- rate_one: bfloat16 [16384, 8], P(('head', 'tok')), may hold values from 0.099609375 to 1
- query_two: bfloat16 [16384, 4096], P(('head', 'tok')), may hold values from -6 to 6
- w_gate: float32 [8, 512, 512], P('head', 'tok'), may hold values from -0.25 to 0.25
- w_up: float32 [8, 512, 512], P('head', 'tok'), may hold values from -0.25 to 0.25
- w_down: float32 [8, 512, 512], P('head', 'tok'), may hold values from -0.25 to 0.25
- step_size: float32 [8], P('head'), may hold values from 0.02 to 0.08
Outputs:
- out_one: bfloat16 [16384, 4096], P(('head', 'tok'))
- out_two: bfloat16 [16384, 4096], P(('head', 'tok'))
- gate_new: float32 [8, 512, 512], P('head', 'tok')
- up_new: float32 [8, 512, 512], P('head', 'tok')
- down_new: float32 [8, 512, 512], P('head', 'tok')
All inputs are finite; a program needn't handle non-finite values.
Results may differ from a plain program's by a relative error of at most 0.011.
Values may be sent and summed in bfloat16 or wider, within the bound.
A program may use at most 64 MiB of HBM per device.

v0:
```python
import jax
import jax.numpy as jnp
from jax import lax
from jax.sharding import PartitionSpec as P


def apply_piece(query, gate_b, up_b, down_b):
    pre_gate = jnp.einsum("thd,hjd->htj", query, gate_b, preferred_element_type=jnp.float32)
    pre_up = jnp.einsum("thd,hjd->htj", query, up_b, preferred_element_type=jnp.float32)
    hidden = (pre_gate * jax.nn.sigmoid(pre_gate) * pre_up).astype(jnp.bfloat16)
    return jnp.einsum("htj,hjd->thd", hidden, down_b, preferred_element_type=jnp.float32)


def forward_piece(query, keys, targets, gate_b, up_b, down_b):
    out_term = apply_piece(query, gate_b, up_b, down_b)
    key_gate = jnp.einsum("thd,hjd->htj", keys, gate_b, preferred_element_type=jnp.float32)
    key_up = jnp.einsum("thd,hjd->htj", keys, up_b, preferred_element_type=jnp.float32)
    sigmoid_k = jax.nn.sigmoid(key_gate)
    act_k = key_gate * sigmoid_k
    hidden_k = (act_k * key_up).astype(jnp.bfloat16)
    back = jnp.einsum("thd,hjd->htj", targets, down_b, preferred_element_type=jnp.float32)
    grad_gate_pre = (back * key_up * sigmoid_k * (1.0 + key_gate * (1.0 - sigmoid_k))).astype(
        jnp.bfloat16
    )
    grad_up_pre = (back * act_k).astype(jnp.bfloat16)
    return (out_term, grad_gate_pre, grad_up_pre, hidden_k)


def gradient_rows(gate_all, up_all, hidden_all, keys, targets):
    grad_gate = jnp.einsum("htj,thd->jhd", gate_all, keys, preferred_element_type=jnp.float32)
    grad_up = jnp.einsum("htj,thd->jhd", up_all, keys, preferred_element_type=jnp.float32)
    grad_down = jnp.einsum("htj,thd->jhd", hidden_all, targets, preferred_element_type=jnp.float32)
    return jnp.stack([grad_gate, grad_up, grad_down], axis=2)


def renew(weights, grad_rows, step_size):
    grads = jnp.moveaxis(grad_rows, 0, 1)
    scale = jnp.sqrt(jnp.mean(grads * grads, axis=2, keepdims=True) + 1e-06)
    return weights - step_size[:, None, None] * grads / scale


def local(query_one, key_one, value_one, rate_one, query_two, w_gate, w_up, w_down, step_size):
    heads_local = w_gate.shape[0]
    width = w_gate.shape[2]
    moved = (
        lax.all_to_all(query_one, "head", split_axis=1, concat_axis=0, tiled=True),
        lax.all_to_all(key_one, "head", split_axis=1, concat_axis=0, tiled=True),
        lax.all_to_all(value_one, "head", split_axis=1, concat_axis=0, tiled=True),
        lax.all_to_all(rate_one, "head", split_axis=1, concat_axis=0, tiled=True),
        lax.all_to_all(query_two, "head", split_axis=1, concat_axis=0, tiled=True),
    )
    tokens = moved[0].shape[0]
    query_a = moved[0].reshape(tokens, heads_local, width)
    keys = moved[1].reshape(tokens, heads_local, width)
    values = moved[2].reshape(tokens, heads_local, width)
    rates = moved[3].astype(jnp.float32)
    query_b = moved[4].reshape(tokens, heads_local, width)
    targets = (-(rates[:, :, None] * values.astype(jnp.float32))).astype(jnp.bfloat16)
    pieces = (
        lax.all_gather(w_gate.astype(jnp.bfloat16), "tok", axis=1, tiled=True),
        lax.all_gather(w_up.astype(jnp.bfloat16), "tok", axis=1, tiled=True),
        lax.all_gather(w_down.astype(jnp.bfloat16), "tok", axis=1, tiled=True),
    )
    out_term, grad_gate_pre, grad_up_pre, hidden_k = forward_piece(
        query_a, keys, targets, pieces[0], pieces[1], pieces[2]
    )
    first_block = out_term.reshape(tokens, heads_local * width).astype(jnp.bfloat16)
    grad_local = lax.psum_scatter(
        gradient_rows(grad_gate_pre, grad_up_pre, hidden_k, keys, targets),
        "tok",
        scatter_dimension=0,
        tiled=True,
    )
    gate_new = renew(w_gate, grad_local[:, :, 0, :], step_size)
    up_new = renew(w_up, grad_local[:, :, 1, :], step_size)
    down_new = renew(w_down, grad_local[:, :, 2, :], step_size)
    pieces = (
        lax.all_gather(gate_new.astype(jnp.bfloat16), "tok", axis=1, tiled=True),
        lax.all_gather(up_new.astype(jnp.bfloat16), "tok", axis=1, tiled=True),
        lax.all_gather(down_new.astype(jnp.bfloat16), "tok", axis=1, tiled=True),
    )
    second_total = apply_piece(query_b, pieces[0], pieces[1], pieces[2])
    second_block = second_total.reshape(tokens, heads_local * width).astype(jnp.bfloat16)
    first_back, second_back = (
        lax.all_to_all(first_block, "head", split_axis=0, concat_axis=1, tiled=True),
        lax.all_to_all(second_block, "head", split_axis=0, concat_axis=1, tiled=True),
    )
    return (first_back, second_back, gate_new, up_new, down_new)


def solution(mesh):
    in_specs = (
        P(("head", "tok"), None),
        P(("head", "tok"), None),
        P(("head", "tok"), None),
        P(("head", "tok"), None),
        P(("head", "tok"), None),
        P("head", "tok", None),
        P("head", "tok", None),
        P("head", "tok", None),
        P("head"),
    )
    out_specs = (
        P(("head", "tok"), None),
        P(("head", "tok"), None),
        P("head", "tok", None),
        P("head", "tok", None),
        P("head", "tok", None),
    )
    return jax.shard_map(local, mesh=mesh, in_specs=in_specs, out_specs=out_specs, check_vma=False)
```

profile of v0, /device:TPU:1, one launch (start us, length us, event | category | flops | bytes accessed | tf_op | source)
XLA Modules:
  0.0 1364.1 jit_solution(18135310961557693874)
XLA Ops:
  7.2 1.3 copy.43
  8.4 10.1 all-to-all-start.2
  19.3 76.5 %all_gather.20 = bf16[1,512,512]{2,1,0:T(8,128)(2,1)S(1)} all-gather(bf16[1,8,512]{2,1,0:T(8,128)(2,1)S(1)} %convert_element_type.143), channel_id=1, replica_groups=mesh['head'=8,'tok'=64] {'tok'}, dimensions={1}, use_global_device_ids=true | all-gather | bytes 532480 | tf_op jit(solution)/shard_map/all_gather | solution.py:62
  96.5 73.1 %all_gather.19 = bf16[1,512,512]{2,1,0:T(8,128)(2,1)S(1)} all-gather(bf16[1,8,512]{2,1,0:T(8,128)(2,1)S(1)} %convert_element_type.141), channel_id=1, replica_groups=mesh['head'=8,'tok'=64] {'tok'}, dimensions={1}, use_global_device_ids=true | all-gather | bytes 532480 | tf_op jit(solution)/shard_map/all_gather | solution.py:61
  170.4 1.7 copy.66
  172.0 1.7 copy.65
  173.7 55.9 %all-to-all-start.4 = ((bf16[32,8,512]{2,0,1:T(8,128)(2,1)}), bf16[32,8,512]{2,0,1:T(8,128)(2,1)S(1)}, u32[]{:S(2)}, u32[]{:S(2)}) async-start(bf16[32,8,512]{2,0,1:T(8,128)(2,1)} %bitcast.139), calls=%async_computation.4 | async-start | bytes 524288 | tf_op jit(solution)/shard_map/all_to_all | solution.py:47
  229.7 71.9 %all_gather.18 = bf16[1,512,512]{2,1,0:T(8,128)(2,1)S(1)} all-gather(bf16[1,8,512]{2,1,0:T(8,128)(2,1)S(1)} %convert_element_type.140), channel_id=1, replica_groups=mesh['head'=8,'tok'=64] {'tok'}, dimensions={1}, use_global_device_ids=true | all-gather | bytes 532480 | tf_op jit(solution)/shard_map/all_gather | solution.py:60
  301.7 30.4 %all-to-all-start.3 = ((bf16[32,8,512]{2,0,1:T(8,128)(2,1)}), bf16[32,8,512]{2,0,1:T(8,128)(2,1)S(1)}, u32[]{:S(2)}, u32[]{:S(2)}) async-start(bf16[32,8,512]{2,0,1:T(8,128)(2,1)} %bitcast.140), calls=%async_computation.3 | async-start | bytes 524288 | tf_op jit(solution)/shard_map/all_to_all | solution.py:48
  332.7 5.8 all-to-all-done.3
  340.3 1.9 pad_maximum_fusion
  343.9 4.4 all-to-all-start
  349.7 5.1 all-to-all-done
  354.8 4.4 all-to-all-start.5
  360.7 665.9 %reduce-scatter.2.cloned.1.call-done = f32[8,1,3,512]{3,0,2,1:T(8,128)} async-done(((f32[512,1,3,512]{3,0,2,1:T(8,128)}), f32[8,1,3,512]{3,0,2,1:T(8,128)}) %reduce-scatter.2.cloned.1.call-update) | async-done | bytes 49168 | tf_op jit(solution)/shard_map/reduce_scatter | solution.py:68
  1027.6 1.5 fusion.47
  1029.0 72.6 %all_gather.23 = bf16[1,512,512]{2,1,0:T(8,128)(2,1)S(1)} all-gather(bf16[1,8,512]{2,1,0:T(8,128)(2,1)S(1)} %get-tuple-element.14), channel_id=1, replica_groups=mesh['head'=8,'tok'=64] {'tok'}, dimensions={1}, use_global_device_ids=true | all-gather | bytes 532480 | tf_op jit(solution)/shard_map/all_gather | solution.py:79
  1101.6 73.4 %all_gather.21 = bf16[1,512,512]{2,1,0:T(8,128)(2,1)S(1)} all-gather(bf16[1,8,512]{2,1,0:T(8,128)(2,1)S(1)} %get-tuple-element.16), channel_id=1, replica_groups=mesh['head'=8,'tok'=64] {'tok'}, dimensions={1}, use_global_device_ids=true | all-gather | bytes 532480 | tf_op jit(solution)/shard_map/all_gather | solution.py:80
  1175.0 72.8 %all_gather.22 = bf16[1,512,512]{2,1,0:T(8,128)(2,1)S(1)} all-gather(bf16[1,8,512]{2,1,0:T(8,128)(2,1)S(1)} %get-tuple-element.8), channel_id=1, replica_groups=mesh['head'=8,'tok'=64] {'tok'}, dimensions={1}, use_global_device_ids=true | all-gather | bytes 532480 | tf_op jit(solution)/shard_map/all_gather | solution.py:78
  1247.8 91.3 %all-to-all-start.1 = ((bf16[8,32,512]{2,1,0:T(8,128)(2,1)}), bf16[8,32,512]{2,1,0:T(8,128)(2,1)S(1)}, u32[]{:S(2)}, u32[]{:S(2)}) async-start(bf16[8,32,512]{2,1,0:T(8,128)(2,1)} %bitcast.9), calls=%async_computation.1 | async-start | bytes 524288 | tf_op jit(solution)/shard_map/all_to_all | solution.py:85
  1339.5 1.3 convolution_convert_fusion
  1340.7 4.9 all-to-all-done.1
  1345.6 4.4 all-to-all-start.6
  1350.7 5.8 all-to-all-done.6
  (38 shorter events, 11.3 us)
Async XLA Ops:
  8.4 165.3 %all-to-all-start.2 = ((bf16[32,8,1]{0,2,1:T(2,128)(2,1)}), bf16[32,8,1]{0,2,1:T(2,128)(2,1)S(1)}, u32[]{:S(2)}, u32[]{:S(2)}) async-start(bf16[32,8,1]{0,2,1:T(2,128)(2,1)} %copy.43), calls=%async_computation.2 | async-start | bytes 8192 | tf_op jit(solution)/shard_map/all_to_all | solution.py:49
  173.7 128.0 %all-to-all-start.4 = ((bf16[32,8,512]{2,0,1:T(8,128)(2,1)}), bf16[32,8,512]{2,0,1:T(8,128)(2,1)S(1)}, u32[]{:S(2)}, u32[]{:S(2)}) async-start(bf16[32,8,512]{2,0,1:T(8,128)(2,1)} %bitcast.139), calls=%async_computation.4 | async-start | bytes 524288 | tf_op jit(solution)/shard_map/all_to_all | solution.py:47
  301.7 36.9 %all-to-all-start.3 = ((bf16[32,8,512]{2,0,1:T(8,128)(2,1)}), bf16[32,8,512]{2,0,1:T(8,128)(2,1)S(1)}, u32[]{:S(2)}, u32[]{:S(2)}) async-start(bf16[32,8,512]{2,0,1:T(8,128)(2,1)} %bitcast.140), calls=%async_computation.3 | async-start | bytes 524288 | tf_op jit(solution)/shard_map/all_to_all | solution.py:48
  332.0 694.6 %reduce-scatter.2.cloned.1.call-start = ((), (), s32[]{:S(2)}) async-start(), calls=%async_computation.8 | async-start | bytes 3194880 | tf_op jit(solution)/shard_map/reduce_scatter | solution.py:68
  342.2 0.9 copy-start
  342.2 6.0 copy-start.1
  343.9 10.9 all-to-all-start
  348.3 679.3 %copy-start.2 = (f32[1,8,512]{2,1,0:T(8,128)S(1)}, f32[1,8,512]{2,1,0:T(8,128)}, u32[]{:S(2)}) copy-start(f32[1,8,512]{2,1,0:T(8,128)} %param.16) | copy-start | bytes 49156
  348.3 679.3 %copy-start.3 = (f32[1,8,512]{2,1,0:T(8,128)S(1)}, f32[1,8,512]{2,1,0:T(8,128)}, u32[]{:S(2)}) copy-start(f32[1,8,512]{2,1,0:T(8,128)} %param.15) | copy-start | bytes 49156
  348.3 679.3 %copy-start.4 = (f32[1,8,512]{2,1,0:T(8,128)S(1)}, f32[1,8,512]{2,1,0:T(8,128)}, u32[]{:S(2)}) copy-start(f32[1,8,512]{2,1,0:T(8,128)} %param.14) | copy-start | bytes 49156
  354.8 893.0 %all-to-all-start.5 = ((bf16[32,8,512]{2,0,1:T(8,128)(2,1)}), bf16[32,8,512]{2,0,1:T(8,128)(2,1)S(1)}, u32[]{:S(2)}, u32[]{:S(2)}) async-start(bf16[32,8,512]{2,0,1:T(8,128)(2,1)} %bitcast.138), calls=%async_computation.6 | async-start | bytes 524288 | tf_op jit(solution)/shard_map/all_to_all | solution.py:50
  1247.8 97.8 %all-to-all-start.1 = ((bf16[8,32,512]{2,1,0:T(8,128)(2,1)}), bf16[8,32,512]{2,1,0:T(8,128)(2,1)S(1)}, u32[]{:S(2)}, u32[]{:S(2)}) async-start(bf16[8,32,512]{2,1,0:T(8,128)(2,1)} %bitcast.9), calls=%async_computation.1 | async-start | bytes 524288 | tf_op jit(solution)/shard_map/all_to_all | solution.py:85
  1345.6 10.9 all-to-all-start.6
Sparse Core Ops, SparseCore 0:
  342.4 684.1 reduce-scatter.1
where the time goes:
time: 1370 us; the launch traced here: 1360 us
  waiting for transfers between devices  688 us (50%)
  blocking collectives  440 us (32%)
  starting transfers between devices  201 us (15%)
  between operations  14.8 us (1%)
    reduce_scatter x1, waiting for transfers between devices, local(): lax.psum_scatter(gradient_rows(grad_gate_pre, grad_up_pre, hidden_k, keys...  666 us
    all_to_all x1, starting transfers between devices, local(): lax.all_to_all(first_block, 'head', split_axis=0, concat_axis=1, tiled=True)  91.3 us
    all_gather x1, blocking collectives, local(): lax.all_gather(w_down.astype(jnp.bfloat16), 'tok', axis=1, tiled=True)  76.5 us
    all_gather x1, blocking collectives, local(): lax.all_gather(down_new.astype(jnp.bfloat16), 'tok', axis=1, tiled=True)  73.4 us
    all_gather x1, blocking collectives, local(): lax.all_gather(w_up.astype(jnp.bfloat16), 'tok', axis=1, tiled=True)  73.1 us
    all_gather x1, blocking collectives, local(): lax.all_gather(gate_new.astype(jnp.bfloat16), 'tok', axis=1, tiled=True)  72.8 us
    all_gather x1, blocking collectives, local(): lax.all_gather(up_new.astype(jnp.bfloat16), 'tok', axis=1, tiled=True)  72.6 us
    all_gather x1, blocking collectives, local(): lax.all_gather(w_gate.astype(jnp.bfloat16), 'tok', axis=1, tiled=True)  71.9 us
  transfers between devices with their start and end apart: 8, of which 5 were waited for; matrix products, arithmetic and copies ran while one was open for 1% of the time, Pallas kernels for 0%

commit v1 on v0

v1 whole, which is shorter than its diff:
```python
import functools

import jax
import jax.numpy as jnp
from jax import lax
from jax.experimental import pallas as pl
from jax.experimental.pallas import tpu as pltpu
from jax.sharding import PartitionSpec as P

MESH = pl.DeviceIdType.MESH
F32 = jnp.float32
BF16 = jnp.bfloat16
WIDTH = 512
COPIES = 96


def dot_nt(a, b):
    return lax.dot_general(a, b, (((1,), (1,)), ((), ())), preferred_element_type=F32)


def dot_nn(a, b):
    return lax.dot_general(a, b, (((1,), (0,)), ((), ())), preferred_element_type=F32)


def kernel(
    step_ref,
    query_one,
    key_one,
    value_one,
    rate_one,
    query_two,
    w_gate,
    w_up,
    w_down,
    out_one,
    out_two,
    gate_new,
    up_new,
    down_new,
    shard,
    shard_in,
    weights,
    moved,
    negated,
    back_one,
    back_two,
    sums,
    wide_in,
    narrow,
    narrow_in,
    last,
    last_in,
    send_sem,
    recv_sem,
    own_sem,
):
    head = lax.axis_index("head")
    tok = lax.axis_index("tok")
    y = lax.rem(tok, 4)
    z = lax.div(tok, 4)
    low = lax.rem(z, 4)
    high = lax.div(z, 4)

    def at_z(distance):
        return (head, lax.rem(z + 16 + distance, 16) * 4 + y)

    def at_y(distance):
        return (head, z * 4 + lax.rem(y + distance, 4))

    def at_head(distance):
        return (lax.rem(head + distance, 8), tok)

    peers = (
        [at_head(i) for i in range(1, 8)]
        + [at_y(i) for i in range(1, 4)]
        + [at_z(i) for i in (1, -1, 2, -2, 4, 8, 12)]
    )
    count = [0]
    sent = []

    def send(src, dst, peer):
        slot = count[0]
        count[0] += 1
        copy = pltpu.make_async_remote_copy(
            src_ref=src,
            dst_ref=dst,
            send_sem=send_sem.at[slot],
            recv_sem=recv_sem.at[slot],
            device_id=peer,
            device_id_type=MESH,
        )
        copy.start()
        sent.append(copy)
        return copy

    def arrive(copies):
        for copy in copies:
            copy.wait_recv()

    def columns(ref, owner):
        return ref.at[:, pl.ds(pl.multiple_of(owner * WIDTH, WIDTH), WIDTH)]

    def spread(ref, which):
        return [
            send(
                columns(ref, lax.rem(head + i, 8)),
                moved.at[which, head],
                at_head(i),
            )
            for i in range(1, 8)
        ]

    def gather_far(g):
        return [send(shard.at[g], shard_in.at[g, j - 1], at_z(4 * j)) for j in (1, 2, 3)]

    def place(g, value, owner_high):
        part = lax.div(owner_high, 2)
        first = jnp.where(part == 0, y, low)
        second = jnp.where(part == 0, low, y)

        @pl.when(lax.rem(owner_high, 2) == 0)
        def _():
            weights[g, part, first, second, :, 0:8, :] = value

        @pl.when(lax.rem(owner_high, 2) == 1)
        def _():
            weights[g, part, first, second, :, 8:16, :] = value

    def gather_rest(g, far):
        place(g, shard[g], high)
        for j in (1, 2, 3):
            far[j - 1].wait_recv()
            place(g, shard_in[g, j - 1], lax.rem(high + 4 - j, 4))
        a = weights.at[g, 0, y, low]
        c = weights.at[g, 1, low, y]
        a2 = [
            send(a, a, at_z(1)),
            send(a, a, at_z(-1)),
            send(a.at[:, :, 0:256], a.at[:, :, 0:256], at_z(2)),
            send(a.at[:, :, 256:512], a.at[:, :, 256:512], at_z(-2)),
        ]
        c2 = [send(c, c, at_y(i)) for i in (1, 2, 3)]
        arrive(a2)
        a = weights.at[g, 0, y]
        a3 = [send(a, a, at_y(i)) for i in (1, 2, 3)]
        arrive(c2)
        c = weights.at[g, 1, low]
        c3 = [
            send(c, c, at_z(1)),
            send(c, c, at_z(-1)),
            send(c.at[0:2], c.at[0:2], at_z(2)),
            send(c.at[2:4], c.at[2:4], at_z(-2)),
        ]
        return a3, c3

    def matrix(g, part, which):
        return weights[g, part, :, :, which].reshape(256, WIDTH)

    def tokens(which):
        return moved[which].reshape(256, WIDTH)

    def hidden_of(query, g, part):
        pre_gate = dot_nt(query, matrix(g, part, 0))
        pre_up = dot_nt(query, matrix(g, part, 1))
        return (pre_gate * jax.nn.sigmoid(pre_gate) * pre_up).astype(BF16)

    def apply(which, g, result):
        query = tokens(which)
        total = dot_nn(hidden_of(query, g, 0), matrix(g, 0, 2))
        total += dot_nn(hidden_of(query, g, 1), matrix(g, 1, 2))
        result[...] = total.astype(BF16).reshape(8, 32, WIDTH)

    def give_back(result, out):
        copies = [
            send(result.at[lax.rem(head + i, 8)], columns(out, head), at_head(i))
            for i in range(1, 8)
        ]
        own = pltpu.make_async_copy(result.at[head], columns(out, head), own_sem)
        own.start()
        own.wait()
        return copies

    shard[0, 0] = w_gate[0].astype(BF16)
    shard[0, 1] = w_up[0].astype(BF16)
    shard[0, 2] = w_down[0].astype(BF16)

    barrier = pltpu.get_barrier_semaphore()
    for peer in peers:
        pl.semaphore_signal(barrier, inc=1, device_id=peer, device_id_type=MESH)
    pl.semaphore_wait(barrier, len(peers))

    far = gather_far(0)
    keys_in = spread(key_one, 0)
    for h in range(8):
        block = pl.ds(h * WIDTH, WIDTH)
        rate = rate_one[:, h : h + 1].astype(F32)
        negated[:, block] = (-(rate * value_one[:, block].astype(F32))).astype(BF16)
    targets_in = spread(negated, 1)
    mine = pl.ds(pl.multiple_of(head * WIDTH, WIDTH), WIDTH)
    moved[0, head] = key_one[:, mine]
    moved[1, head] = negated[:, mine]
    moved[2, head] = query_one[:, mine]
    moved[3, head] = query_two[:, mine]

    a3, c3 = gather_rest(0, far)
    arrive(keys_in)
    arrive(targets_in)
    query_one_in = spread(query_one, 2)
    query_two_in = spread(query_two, 3)

    def gradients(part):
        keys, targets = tokens(0), tokens(1)
        gate, up, down = (matrix(0, part, i) for i in range(3))
        key_gate = dot_nt(gate, keys)
        key_up = dot_nt(up, keys)
        back = dot_nt(down, targets)
        sig = jax.nn.sigmoid(key_gate)
        act = key_gate * sig
        hidden = (act * key_up).astype(BF16)
        gate_pre = (back * key_up * sig * (1.0 + key_gate * (1.0 - sig))).astype(BF16)
        up_pre = (back * act).astype(BF16)
        for which, (left, right) in enumerate(
            ((gate_pre, keys), (up_pre, keys), (hidden, targets))
        ):
            total = dot_nn(left, right).astype(BF16)
            sums[part, :, :, which] = total.reshape(4, 4, 16, WIDTH)

    arrive(a3)
    gradients(0)
    a1 = [
        send(sums.at[0, lax.rem(y + i, 4)], wide_in.at[0, i - 1], at_y(i)) for i in (1, 2, 3)
    ]
    arrive(c3)
    gradients(1)

    def near(src, dst, split):
        ahead, behind, across = (lax.rem(low + i, 4) for i in (1, 3, 2))
        return [
            send(src.at[ahead], dst.at[0], at_z(1)),
            send(src.at[behind], dst.at[1], at_z(-1)),
            send(split(src.at[across], 0), split(dst.at[2], 0), at_z(2)),
            send(split(src.at[across], 1), split(dst.at[2], 1), at_z(-2)),
        ]

    c1 = near(sums.at[1], wide_in.at[1], lambda ref, i: ref.at[pl.ds(2 * i, 2)])

    arrive(query_one_in)
    apply(2, 0, back_one)
    one_out = give_back(back_one, out_one)

    def add_wide(part, own):
        for i in range(4):
            total = sums[part, own, i].astype(F32)
            for j in range(3):
                total += wide_in[part, j, i].astype(F32)
            narrow[part, i] = total.astype(BF16)

    arrive(a1)
    add_wide(0, y)
    a2 = near(
        narrow.at[0], narrow_in.at[0], lambda ref, i: ref.at[:, :, pl.ds(256 * i, 256)]
    )
    arrive(c1)
    add_wide(1, low)
    c2 = [
        send(narrow.at[1, lax.rem(y + i, 4)], narrow_in.at[1, i - 1], at_y(i))
        for i in (1, 2, 3)
    ]

    def add_narrow(part, own):
        total = narrow[part, own].astype(F32)
        for j in range(3):
            total += narrow_in[part, j].astype(F32)
        last[2 * part] = total[:, 0:8].astype(BF16)
        last[2 * part + 1] = total[:, 8:16].astype(BF16)

    arrive(a2)
    add_narrow(0, low)
    arrive(c2)
    add_narrow(1, y)
    final = [
        send(last.at[lax.rem(high + j, 4)], last_in.at[j - 1], at_z(4 * j)) for j in (1, 2, 3)
    ]
    total = last[high].astype(F32)
    arrive(final)
    for j in range(3):
        total += last_in[j].astype(F32)

    step = step_ref[0]
    for which, (old, new) in enumerate(
        ((w_gate, gate_new), (w_up, up_new), (w_down, down_new))
    ):
        grads = total[which]
        scale = jnp.sqrt(jnp.mean(grads * grads, axis=1, keepdims=True) + 1e-06)
        renewed = old[0] - step * grads / scale
        new[0] = renewed
        shard[1, which] = renewed.astype(BF16)

    far = gather_far(1)
    a3, c3 = gather_rest(1, far)
    arrive(query_two_in)
    arrive(a3)
    arrive(c3)
    apply(3, 1, back_two)
    two_out = give_back(back_two, out_two)
    arrive(one_out)
    arrive(two_out)
    for copy in sent:
        copy.wait_send()


def local(query_one, key_one, value_one, rate_one, query_two, w_gate, w_up, w_down, step_size):
    vmem = pl.BlockSpec(memory_space=pltpu.VMEM)
    smem = pl.BlockSpec(memory_space=pltpu.SMEM)
    hbm = pl.BlockSpec(memory_space=pl.ANY)
    wide = (4, 3, 16, WIDTH)
    return pl.pallas_call(
        kernel,
        out_shape=(
            jax.ShapeDtypeStruct(query_one.shape, BF16),
            jax.ShapeDtypeStruct(query_one.shape, BF16),
            jax.ShapeDtypeStruct(w_gate.shape, F32),
            jax.ShapeDtypeStruct(w_gate.shape, F32),
            jax.ShapeDtypeStruct(w_gate.shape, F32),
        ),
        in_specs=[smem] + [vmem] * 8,
        out_specs=(vmem,) * 5,
        scratch_shapes=[
            pltpu.VMEM((2, 3, 8, WIDTH), BF16),
            pltpu.VMEM((2, 3, 3, 8, WIDTH), BF16),
            pltpu.VMEM((2, 2, 4) + wide, BF16),
            pltpu.VMEM((4, 8, 32, WIDTH), BF16),
            pltpu.VMEM((32, 8 * WIDTH), BF16),
            pltpu.VMEM((8, 32, WIDTH), BF16),
            pltpu.VMEM((8, 32, WIDTH), BF16),
            pltpu.VMEM((2, 4) + wide, BF16),
            pltpu.VMEM((2, 3) + wide, BF16),
            pltpu.VMEM((2,) + wide, BF16),
            pltpu.VMEM((2, 3, 3, 16, WIDTH), BF16),
            pltpu.VMEM((4, 3, 8, WIDTH), BF16),
            pltpu.VMEM((3, 3, 8, WIDTH), BF16),
            pltpu.SemaphoreType.DMA((COPIES,)),
            pltpu.SemaphoreType.DMA((COPIES,)),
            pltpu.SemaphoreType.DMA,
        ],
        compiler_params=pltpu.CompilerParams(
            collective_id=0, has_side_effects=True, vmem_limit_bytes=48 * 1024 * 1024
        ),
        cost_estimate=pl.CostEstimate(
            flops=1700000000, bytes_accessed=2000000, transcendentals=400000
        ),
    )(step_size, query_one, key_one, value_one, rate_one, query_two, w_gate, w_up, w_down)


def solution(mesh):
    rows = P(("head", "tok"), None)
    shards = P("head", "tok", None)
    return jax.shard_map(
        local,
        mesh=mesh,
        in_specs=(rows,) * 5 + (shards,) * 3 + (P("head"),),
        out_specs=(rows,) * 2 + (shards,) * 3,
        check_vma=False,
    )
```

time: 1370 us -> 107 us (0.08)
  the two profiles are of different devices: /device:TPU:1 before, /device:TPU:17 now
where the time goes in v1:
time: 107 us; the launch traced here: 106 us
  Pallas kernels  95.1 us (89%)
  local copies, waits for them, and re-layouts  9.94 us (9%)
  between operations  1.3 us (1%)
    pallas_call x1, Pallas kernels, local(): pl.pallas_call(kernel, out_shape=(jax.ShapeDtypeStruct(query_one.shape, B...  95.1 us
    unnamed x20, local copies, waits for them, and re-layouts  9.94 us

profile of v1, /device:TPU:17, one launch (start us, length us, event | category | flops | bytes accessed | tf_op | source)
XLA Modules:
  0.0 106.3 jit_solution(619623061875779967)
XLA Ops:
  1.3 0.8 copy.14.rate_one
  2.0 0.0 copy-start
  2.0 0.9 copy-done
  3.0 0.0 copy-start.1
  3.0 0.9 copy-done.1
  3.9 0.0 copy-start.2
  3.9 0.9 copy-done.2
  4.9 0.0 copy-start.3
  4.9 0.9 copy-done.3
  5.8 0.0 copy-start.4
  5.8 0.7 copy-done.4
  6.6 0.0 copy-start.5
  6.6 0.7 copy-done.5
  7.3 0.0 copy-start.6
  7.3 0.7 copy-done.6
  8.0 95.1 %shard_map.128 = (bf16[32,4096]{1,0:T(8,128)(2,1)S(1)}, bf16[32,4096]{1,0:T(8,128)(2,1)S(1)}, f32[1,8,512]{2,1,0:T(8,128)S(1)}, f32[1,8,512]{2,1,0:T(8,128)S(1)}, f32[1,8,512]{2,1,0:T(8,128)S(1)}) custom-call(f32[1]{0:T(128)S(6)} %copy.20.step_ref, bf16[32,4096]{1,0:T(8,128)(2,1)S(1)} %copy-done, bf16[32,4096]{1,0:T(8,128)(2,1)S(1)} %copy-done.1, ...), custom_call_target="tpu_custom_call" | custom-call | flops 1700000000 | bytes 2000000 | tf_op jit(solution)/shard_map/pallas_call | solution.py:317
  103.1 0.7 copy.21
  103.8 0.7 copy.22
  104.5 0.6 copy.23
  105.1 0.6 copy.24
  105.7 0.6 copy.25
Async XLA Ops:
  2.0 1.0 copy-start
  3.0 0.9 copy-start.1
  3.9 0.9 copy-start.2
  4.9 0.9 copy-start.3
  5.8 0.7 copy-start.4
  6.6 0.7 copy-start.5
  7.3 0.7 copy-start.6

commit v2 on v1

v2 whole, which is shorter than its diff:
```python
import jax
import jax.numpy as jnp
from jax import lax
from jax.experimental import pallas as pl
from jax.experimental.pallas import tpu as pltpu
from jax.sharding import PartitionSpec as P

MESH = pl.DeviceIdType.MESH
F32 = jnp.float32
BF16 = jnp.bfloat16
WIDTH = 512
COPIES = 128
PAIRS = ((0, 2), (1, 3))


def dot_nt(a, b):
    return lax.dot_general(a, b, (((1,), (1,)), ((), ())), preferred_element_type=F32)


def dot_nn(a, b):
    return lax.dot_general(a, b, (((1,), (0,)), ((), ())), preferred_element_type=F32)


def kernel(
    step_ref,
    rate_turned,
    query_one,
    key_one,
    value_hbm,
    query_two,
    w_gate_hbm,
    w_up_hbm,
    w_down_hbm,
    out_one,
    out_two,
    gate_new,
    up_new,
    down_new,
    value_one,
    w_own,
    fresh,
    shard,
    shard_in,
    near_in,
    weights,
    moved,
    negated,
    back_one,
    back_two,
    sums,
    wide_in,
    narrow,
    narrow_in,
    last,
    last_in,
    send_sem,
    recv_sem,
    load_sem,
    own_sem,
):
    head = lax.axis_index("head")
    tok = lax.axis_index("tok")
    y = lax.rem(tok, 4)
    z = lax.div(tok, 4)
    low = lax.rem(z, 4)
    high = lax.div(z, 4)

    def tok_z(distance):
        return lax.rem(z + 16 + distance, 16) * 4 + y

    def tok_y(distance):
        return z * 4 + lax.rem(y + distance, 4)

    def at_head(distance):
        return (lax.rem(head + distance, 8), tok)

    def tok_near(distance, u):
        if distance == 2:
            return tok_z(jnp.where(lax.rem(u, 2) == 0, 2, -2))
        return tok_z(1 if distance == 1 else -1)

    def pick(u, a, b):
        if isinstance(u, int):
            return a if u < 2 else b
        return jnp.where(u < 2, a, b)

    def peer_two(distance, u):
        return (head, pick(u, tok_near(distance, u), tok_y(distance)))

    def peer_three(distance, u):
        return (head, pick(u, tok_y(distance), tok_near(distance, u)))

    def first(u):
        return pick(u, y, low)

    def second(u):
        return pick(u, low, y)

    sent = []
    count = [0]

    def block_of_slots(size):
        base = count[0]
        count[0] += size
        return base

    def send(slot, src, dst, peer):
        copy = pltpu.make_async_remote_copy(
            src_ref=src,
            dst_ref=dst,
            send_sem=send_sem.at[slot],
            recv_sem=recv_sem.at[slot],
            device_id=peer,
            device_id_type=MESH,
        )
        copy.start()
        sent.append(copy)
        return copy

    def arrive(copies):
        for copy in copies:
            copy.wait_recv()

    def columns(ref, owner):
        return ref.at[:, pl.ds(pl.multiple_of(owner * WIDTH, WIDTH), WIDTH)]

    def spread(ref, which):
        base = block_of_slots(7)
        return [
            send(base + i - 1, columns(ref, lax.rem(head + i, 8)), moved.at[which, head], at_head(i))
            for i in range(1, 8)
        ]

    def place(g, u, other, value):
        for half in range(2):

            @pl.when(lax.rem(other, 2) == half)
            def _():
                rows = slice(8 * half, 8 * half + 8)
                weights[g, u, first(u), lax.div(other, 2), :, rows, :] = value

    units = [lax.rem(high + 4 - j, 4) for j in (0, 3, 1, 2)]

    def gather(g):
        far_base, two_base, three_base = block_of_slots(3), block_of_slots(12), block_of_slots(12)
        far = {
            j: send(far_base + j - 1, shard.at[g], shard_in.at[g, j - 1], (head, tok_z(4 * j)))
            for j in (2, 1, 3)
        }
        two = []
        for n, j in enumerate((0, 3, 1, 2)):
            u = units[n]
            if j:
                far[j].wait_recv()
            block = shard_in.at[g, j - 1] if j else shard.at[g]
            two.append(
                [
                    send(two_base + u * 3 + d - 1, block, near_in.at[g, u, d - 1], peer_two(d, u))
                    for d in (1, 3, 2)
                ]
            )
            place(g, u, second(u), block[...])
        for n in range(4):
            u = units[n]
            arrive(two[n])
            for d in (1, 2, 3):
                place(g, u, lax.rem(second(u) + 4 - d, 4), near_in[g, u, d - 1])
            block = weights.at[g, u, first(u)]
            for d in (1, 3, 2):
                send(three_base + u * 3 + d - 1, block, block, peer_three(d, u))
        return {
            u: [
                pltpu.make_async_remote_copy(
                    src_ref=weights.at[g, u, first(u)],
                    dst_ref=weights.at[g, u, first(u)],
                    send_sem=send_sem.at[three_base + u * 3 + d - 1],
                    recv_sem=recv_sem.at[three_base + u * 3 + d - 1],
                    device_id=peer_three(d, u),
                    device_id_type=MESH,
                )
                for d in (1, 3, 2)
            ]
            for u in range(4)
        }

    def matrix(g, pair, which):
        return jnp.concatenate(
            [weights[g, u, :, :, which].reshape(128, WIDTH) for u in PAIRS[pair]]
        )

    def tokens(which):
        return moved[which].reshape(256, WIDTH)

    def apply(query, g, pair):
        pre_gate = dot_nt(query, matrix(g, pair, 0))
        pre_up = dot_nt(query, matrix(g, pair, 1))
        hidden = (pre_gate * jax.nn.sigmoid(pre_gate) * pre_up).astype(BF16)
        return dot_nn(hidden, matrix(g, pair, 2))

    def give_back(total, result, out, which):
        result[...] = total.astype(BF16).reshape(8, 32, WIDTH)
        base = block_of_slots(7)
        copies = [
            send(base + i - 1, result.at[lax.rem(head + i, 8)], columns(out, head), at_head(i))
            for i in range(1, 8)
        ]
        own = pltpu.make_async_copy(result.at[head], columns(out, head), own_sem.at[which])
        own.start()
        return copies, own

    loads = [
        pltpu.make_async_copy(src, dst, load_sem.at[i])
        for i, (src, dst) in enumerate(
            (
                (w_gate_hbm.at[0], w_own.at[0]),
                (w_up_hbm.at[0], w_own.at[1]),
                (w_down_hbm.at[0], w_own.at[2]),
                (value_hbm, value_one),
                (columns(key_one, head), moved.at[0, head]),
                (columns(query_one, head), moved.at[2, head]),
                (columns(query_two, head), moved.at[3, head]),
            )
        )
    ]
    for load in loads:
        load.start()

    barrier = pltpu.get_barrier_semaphore()
    peers = [(head, tok_z(i)) for i in (8, 4, 12, 2, -2, 1, -1)]
    peers += [(head, tok_y(i)) for i in (2, 1, 3)]
    peers += [at_head(i) for i in range(1, 8)]
    for peer in peers:
        pl.semaphore_signal(barrier, inc=1, device_id=peer, device_id_type=MESH)
    for load in loads:
        load.wait()
    shard[0] = w_own[...].astype(BF16)
    rates = rate_turned[...].astype(F32).T
    for h in range(8):
        block = pl.ds(h * WIDTH, WIDTH)
        product = rates[:, h : h + 1] * value_one[:, block].astype(F32)
        negated[:, block] = (-product).astype(BF16)
    moved[1, head] = negated[:, pl.ds(pl.multiple_of(head * WIDTH, WIDTH), WIDTH)]
    pl.semaphore_wait(barrier, len(peers))

    keys_in = spread(key_one, 0)
    targets_in = spread(negated, 1)
    gathered = gather(0)
    arrive(keys_in)
    arrive(targets_in)

    def gradients(pair):
        keys, targets = tokens(0), tokens(1)
        gate, up, down = (matrix(0, pair, i) for i in range(3))
        key_gate = dot_nt(gate, keys)
        key_up = dot_nt(up, keys)
        back = dot_nt(down, targets)
        sig = jax.nn.sigmoid(key_gate)
        act = key_gate * sig
        hidden = (act * key_up).astype(BF16)
        gate_pre = (back * key_up * sig * (1.0 + key_gate * (1.0 - sig))).astype(BF16)
        up_pre = (back * act).astype(BF16)
        for which, (left, right) in enumerate(
            ((gate_pre, keys), (up_pre, keys), (hidden, targets))
        ):
            total = dot_nn(left, right).astype(BF16)
            for i in range(2):
                part = total[128 * i : 128 * i + 128].reshape(4, 2, 16, WIDTH)
                sums[PAIRS[pair][i], :, :, which] = part

    one_base, two_base, far_base = block_of_slots(12), block_of_slots(12), block_of_slots(3)
    wide, thin = {}, {}

    def send_wide(u):
        wide[u] = [
            send(
                one_base + u * 3 + d - 1,
                sums.at[u, lax.rem(first(u) + d, 4)],
                wide_in.at[u, d - 1],
                peer_three(d, u),
            )
            for d in (1, 3, 2)
        ]

    def send_thin(u):
        arrive(wide[u])
        for i in range(2):
            total = sums[u, first(u), i].astype(F32)
            for d in range(3):
                total += wide_in[u, d, i].astype(F32)
            narrow[u, 2 * i] = total[:, 0:8].astype(BF16)
            narrow[u, 2 * i + 1] = total[:, 8:16].astype(BF16)
        thin[u] = [
            send(
                two_base + u * 3 + d - 1,
                narrow.at[u, lax.rem(second(u) + d, 4)],
                narrow_in.at[u, d - 1],
                peer_two(d, u),
            )
            for d in (1, 3, 2)
        ]

    def send_last(u):
        arrive(thin[u])
        total = narrow[u, second(u)].astype(F32)
        for d in range(3):
            total += narrow_in[u, d].astype(F32)
        last[u] = total.astype(BF16)
        distance = lax.rem(u + 4 - high, 4)

        @pl.when(distance > 0)
        def _():
            far_copy(u, distance).start()

    def far_copy(u, distance):
        slot = far_base + jnp.maximum(distance, 1) - 1
        return pltpu.make_async_remote_copy(
            src_ref=last.at[u],
            dst_ref=last_in.at[jnp.maximum(distance, 1) - 1],
            send_sem=send_sem.at[slot],
            recv_sem=recv_sem.at[slot],
            device_id=(head, lax.rem(z + 4 * distance, 16) * 4 + y),
            device_id_type=MESH,
        )

    for pair in range(2):
        for u in PAIRS[pair]:
            arrive(gathered[u])
        gradients(pair)
        for u in PAIRS[pair]:
            send_wide(u)
    query_one_in = spread(query_one, 2)
    query_two_in = spread(query_two, 3)
    for u in PAIRS[0]:
        send_thin(u)
    for u in PAIRS[0]:
        send_last(u)
    for u in PAIRS[1]:
        send_thin(u)
    for u in PAIRS[1]:
        send_last(u)
    arrive(query_one_in)
    answer = apply(tokens(2), 0, 0) + apply(tokens(2), 0, 1)
    one_out, one_own = give_back(answer, back_one, out_one, 0)
    total = last[high].astype(F32)
    for j in (1, 3, 2):
        far_copy(lax.rem(high + j, 4), j).wait_recv()
        far_copy(lax.rem(high + j, 4), j).wait_send()
        total += last_in[j - 1].astype(F32)

    step = step_ref[0]
    keep = []
    for which, new in enumerate((gate_new, up_new, down_new)):
        grads = total[which]
        scale = jnp.sqrt(jnp.mean(grads * grads, axis=1, keepdims=True) + 1e-06)
        renewed = w_own[which] - step * grads / scale
        fresh[which] = renewed
        keep.append(pltpu.make_async_copy(fresh.at[which], new.at[0], own_sem.at[which + 2]))
        keep[-1].start()
        shard[1, which] = renewed.astype(BF16)

    gathered = gather(1)
    arrive(query_two_in)
    arrive(gathered[0] + gathered[2])
    answer = apply(tokens(3), 1, 0)
    arrive(gathered[1] + gathered[3])
    answer += apply(tokens(3), 1, 1)
    two_out, two_own = give_back(answer, back_two, out_two, 1)
    for copy in [one_own] + keep + [two_own]:
        copy.wait()
    arrive(one_out)
    arrive(two_out)
    for copy in sent:
        copy.wait_send()


def write_out(*refs):
    sources, targets, held = refs[:5], refs[5:10], refs[10:15]
    sems = refs[15]
    into = [pltpu.make_async_copy(sources[i], held[i], sems.at[0, i]) for i in range(5)]
    out = [pltpu.make_async_copy(held[i], targets[i], sems.at[1, i]) for i in range(5)]
    for copy in into:
        copy.start()
    for i in range(5):
        into[i].wait()
        out[i].start()
    for copy in out:
        copy.wait()


def local(query_one, key_one, value_one, rate_one, query_two, w_gate, w_up, w_down, step_size):
    vmem = pl.BlockSpec(memory_space=pltpu.VMEM)
    smem = pl.BlockSpec(memory_space=pltpu.SMEM)
    hbm = pl.BlockSpec(memory_space=pltpu.HBM)
    whole = (2, 3, 16, WIDTH)
    results = (
        jax.ShapeDtypeStruct(query_one.shape, BF16),
        jax.ShapeDtypeStruct(query_one.shape, BF16),
        jax.ShapeDtypeStruct(w_gate.shape, F32),
        jax.ShapeDtypeStruct(w_gate.shape, F32),
        jax.ShapeDtypeStruct(w_gate.shape, F32),
    )
    made = pl.pallas_call(
        kernel,
        out_shape=results,
        in_specs=[smem, vmem] + [hbm] * 7,
        out_specs=(hbm,) * 5,
        scratch_shapes=[
            pltpu.VMEM((32, 8 * WIDTH), BF16),
            pltpu.VMEM((3, 8, WIDTH), F32),
            pltpu.VMEM((3, 8, WIDTH), F32),
            pltpu.VMEM((2, 3, 8, WIDTH), BF16),
            pltpu.VMEM((2, 3, 3, 8, WIDTH), BF16),
            pltpu.VMEM((2, 4, 3, 3, 8, WIDTH), BF16),
            pltpu.VMEM((2, 4, 4) + whole, BF16),
            pltpu.VMEM((4, 8, 32, WIDTH), BF16),
            pltpu.VMEM((32, 8 * WIDTH), BF16),
            pltpu.VMEM((8, 32, WIDTH), BF16),
            pltpu.VMEM((8, 32, WIDTH), BF16),
            pltpu.VMEM((4, 4) + whole, BF16),
            pltpu.VMEM((4, 3) + whole, BF16),
            pltpu.VMEM((4, 4, 3, 8, WIDTH), BF16),
            pltpu.VMEM((4, 3, 3, 8, WIDTH), BF16),
            pltpu.VMEM((4, 3, 8, WIDTH), BF16),
            pltpu.VMEM((3, 3, 8, WIDTH), BF16),
            pltpu.SemaphoreType.DMA((COPIES,)),
            pltpu.SemaphoreType.DMA((COPIES,)),
            pltpu.SemaphoreType.DMA((7,)),
            pltpu.SemaphoreType.DMA((5,)),
        ],
        compiler_params=pltpu.CompilerParams(
            collective_id=0, has_side_effects=True, vmem_limit_bytes=62 * 1024 * 1024
        ),
        cost_estimate=pl.CostEstimate(
            flops=1700000000, bytes_accessed=2000000, transcendentals=400000
        ),
    )(step_size, rate_one.T, query_one, key_one, value_one, query_two, w_gate, w_up, w_down)
    return pl.pallas_call(
        write_out,
        out_shape=results,
        in_specs=[hbm] * 5,
        out_specs=(hbm,) * 5,
        scratch_shapes=[pltpu.VMEM(made[i].shape, made[i].dtype) for i in range(5)]
        + [pltpu.SemaphoreType.DMA((2, 5))],
        compiler_params=pltpu.CompilerParams(vmem_limit_bytes=62 * 1024 * 1024),
    )(*made)


def solution(mesh):
    rows = P(("head", "tok"), None)
    shards = P("head", "tok", None)
    return jax.shard_map(
        local,
        mesh=mesh,
        in_specs=(rows,) * 5 + (shards,) * 3 + (P("head"),),
        out_specs=(rows,) * 2 + (shards,) * 3,
        check_vma=False,
    )
```

time: 107 us -> 96.8 us (0.905)
  the two profiles are of different devices: /device:TPU:17 before, /device:TPU:1 now
where the time goes in v2:
time: 96.8 us; the launch traced here: 96.6 us
  Pallas kernels  95.3 us (98%)
  between operations  1.29 us (1%)
    pallas_call x1, Pallas kernels, local(): pl.pallas_call(kernel, out_shape=results, in_specs=[smem, vmem] + [hbm] *...  93.4 us

profile of v2, /device:TPU:1, one launch (start us, length us, event | category | flops | bytes accessed | tf_op | source)
XLA Modules:
  0.0 96.6 jit_solution(5964248453544904125)
XLA Ops:
  1.3 93.4 %shard_map.128 = (bf16[32,4096]{1,0:T(8,128)(2,1)}, bf16[32,4096]{1,0:T(8,128)(2,1)}, f32[1,8,512]{2,1,0:T(8,128)}, f32[1,8,512]{2,1,0:T(8,128)}, f32[1,8,512]{2,1,0:T(8,128)}) custom-call(f32[1]{0:T(128)S(6)} %copy.14.step_ref, bf16[8,32]{1,0:T(8,128)(2,1)} %bitcast.1, bf16[32,4096]{1,0:T(8,128)(2,1)} %query_one.1, bf16[32,4096]{1,0:T(8,128)(2,1)} %key_one.1, ...), custom_call_target="tpu_custom_call" | custom-call | flops 1700000000 | bytes 2000000 | tf_op jit(solution)/shard_map/pallas_call | solution.py:402
  94.7 1.8 %shard_map.129 = (bf16[32,4096]{1,0:T(8,128)(2,1)}, bf16[32,4096]{1,0:T(8,128)(2,1)}, f32[1,8,512]{2,1,0:T(8,128)}, f32[1,8,512]{2,1,0:T(8,128)}, f32[1,8,512]{2,1,0:T(8,128)}) custom-call(bf16[32,4096]{1,0:T(8,128)(2,1)} %get-tuple-element.10.refs_0_, bf16[32,4096]{1,0:T(8,128)(2,1)} %get-tuple-element.11.refs_1_, f32[1,8,512]{2,1,0:T(8,128)} %get-tuple-element.12.refs_2_, ...), custom_call_target="tpu_custom_call" | custom-call | tf_op jit(solution)/shard_map/pallas_call | solution.py:437

commit v3 on v2

v3 whole, which is shorter than its diff:
```python
import jax
import jax.numpy as jnp
from jax import lax
from jax.experimental import pallas as pl
from jax.experimental.pallas import tpu as pltpu
from jax.sharding import PartitionSpec as P

MESH = pl.DeviceIdType.MESH
F32 = jnp.float32
BF16 = jnp.bfloat16
WIDTH = 512
COPIES = 136
PAIRS = ((0, 2), (1, 3))


def dot_nt(a, b):
    return lax.dot_general(a, b, (((1,), (1,)), ((), ())), preferred_element_type=F32)


def dot_nn(a, b):
    return lax.dot_general(a, b, (((1,), (0,)), ((), ())), preferred_element_type=F32)


def kernel(
    step_hbm,
    rate_hbm,
    query_one,
    key_one,
    value_hbm,
    query_two,
    w_gate_hbm,
    w_up_hbm,
    w_down_hbm,
    out_one,
    out_two,
    gate_new,
    up_new,
    down_new,
    step_ref,
    rate_turned,
    value_one,
    w_own,
    fresh,
    shard,
    shard_in,
    near_in,
    weights,
    moved,
    negated,
    partial,
    partial_in,
    back,
    sums,
    wide_in,
    narrow,
    narrow_in,
    last,
    last_in,
    send_sem,
    recv_sem,
    load_sem,
    own_sem,
):
    row = lax.axis_index("head")
    tok = lax.axis_index("tok")
    core = lax.rem(row, 2)
    y = lax.rem(tok, 4)
    z = lax.div(tok, 4)
    low, high = lax.rem(z, 4), lax.div(z, 4)
    odd, upper = lax.rem(y, 2), lax.div(y, 2)
    head = row - core + odd
    same = core == odd
    other = core != odd
    owner_y = jnp.where(same, y, y + 1 - 2 * odd)

    def tok_z(distance):
        return lax.rem(z + 16 + distance, 16) * 4 + y

    def near(distance, u):
        if distance == 2:
            return (row, tok_z(jnp.where(lax.rem(u, 2) == 0, 2, -2)))
        return (row, tok_z(1 if distance == 1 else -1))

    across = (row, z * 4 + lax.rem(y + 2, 4))
    sibling = (row + 1 - 2 * core, tok)

    def far(j):
        return (head, lax.rem(z + 4 * j, 16) * 4 + owner_y)

    def at_source(h):
        return (lax.div(h, 2) * 2 + core, z * 4 + upper * 2 + lax.rem(h, 2))

    count = [0]
    ends = []

    def slots(size):
        base = count[0]
        count[0] += size
        return base

    def remote(slot, src, dst, peer):
        return pltpu.make_async_remote_copy(
            src_ref=src,
            dst_ref=dst,
            send_sem=send_sem.at[slot],
            recv_sem=recv_sem.at[slot],
            device_id=peer,
            device_id_type=MESH,
        )

    def send(slot, src, dst, peer):
        copy = remote(slot, src, dst, peer)
        copy.start()
        ends.append(copy)
        return copy

    def arrive(copies):
        for copy in copies:
            copy.wait_recv()

    def columns(ref, h):
        return ref.at[:, pl.ds(pl.multiple_of(h * WIDTH, WIDTH), WIDTH)]

    def spread(ref, which):
        base = slots(7)
        copies = []
        for i in range(1, 8):
            h = lax.rem(head + i, 8)
            copies.append(
                send(base + i - 1, columns(ref, h), moved.at[which, core, head], at_source(h))
            )
        return copies

    def share(copies, which):
        arrive(copies)
        half = moved.at[which, core]
        return [send(slots(1), half, half, sibling)]

    def place(g, u, k, half, value):
        for i in range(2):

            @pl.when(half == i)
            def _():
                weights[g, u, k, :, 8 * i : 8 * i + 8, :] = value

    units = [lax.rem(high + 4 - j, 4) for j in (0, 3, 1, 2)]
    bases = [(slots(4), slots(12), slots(12)) for _ in range(2)]

    def copy_far(g, j):
        return remote(bases[g][0] + j, shard.at[g], shard_in.at[g, j], far(j))

    def copies_two(g, u, j, along_z):
        base = bases[g][1] + u * 3
        block = shard_in.at[g, j]
        if along_z:
            return [
                remote(base + d - 1, block, near_in.at[g, u, d - 1], near(d, u))
                for d in (1, 3, 2)
            ]
        return [remote(base, block, near_in.at[g, u, 0], across)]

    def copies_three(g, u, along_z):
        base = bases[g][2] + u * 3
        if along_z:
            block = weights.at[g, u, low]
            return [remote(base + d - 1, block, block, near(d, u)) for d in (1, 3, 2)]
        block = weights.at[g, u, pl.ds(upper * 2, 2)]
        return [remote(base, block, block, across)]

    def gather_start(g):
        for j in (2, 1, 3):
            copy_far(g, j).start()

        @pl.when(other)
        def _():
            copy_far(g, 0).start()

        @pl.when(same)
        def _():
            shard_in[g, 0] = shard[g]

    def gather_two(g):
        for n, j in enumerate((0, 3, 1, 2)):
            u = units[n]
            if j:
                copy_far(g, j).wait_recv()
            else:

                @pl.when(other)
                def _():
                    copy_far(g, 0).wait_recv()

            @pl.when(u < 2)
            def _():
                for copy in copies_two(g, u, j, True):
                    copy.start()
                place(g, u, upper * 2 + lax.div(low, 2), lax.rem(low, 2), shard_in[g, j])

            @pl.when(u >= 2)
            def _():
                for copy in copies_two(g, u, j, False):
                    copy.start()
                place(g, u, low, upper, shard_in[g, j])

    def gather_three(g):
        for n, j in enumerate((0, 3, 1, 2)):
            u = units[n]

            @pl.when(u < 2)
            def _():
                arrive(copies_two(g, u, j, True))
                for d in (1, 2, 3):
                    s = lax.rem(low + 4 - d, 4)
                    k = upper * 2 + lax.div(s, 2)
                    place(g, u, k, lax.rem(s, 2), near_in[g, u, d - 1])
                for copy in copies_three(g, u, False):
                    copy.start()

            @pl.when(u >= 2)
            def _():
                arrive(copies_two(g, u, j, False))
                place(g, u, low, 1 - upper, near_in[g, u, 0])
                for copy in copies_three(g, u, True):
                    copy.start()

    def gathered(g, u):
        arrive(copies_three(g, u, u >= 2))

    def gather_end(g):
        for j in (1, 2, 3):
            copy_far(g, j).wait_send()

        @pl.when(other)
        def _():
            copy_far(g, 0).wait_send()

        for u in range(4):
            for copy in copies_two(g, u, 0, u < 2) + copies_three(g, u, u >= 2):
                copy.wait_send()

    def matrix(g, chosen, which):
        return jnp.concatenate([weights[g, u, :, which].reshape(64, WIDTH) for u in chosen])

    def apply(which, g, slot, out):
        gate, up, down = (matrix(g, range(4), i) for i in range(3))

        def part(half):
            query = moved[which, half].reshape(256, WIDTH)
            pre_gate = dot_nt(query, gate)
            pre_up = dot_nt(query, up)
            hidden = (pre_gate * jax.nn.sigmoid(pre_gate) * pre_up).astype(BF16)
            return dot_nn(hidden, down)

        partial[slot] = part(1 - core).astype(BF16).reshape(8, 32, WIDTH)
        exchange = send(slots(1), partial.at[slot], partial_in.at[slot], sibling)
        total = part(core)
        exchange.wait_recv()
        total += partial_in[slot].reshape(256, WIDTH).astype(F32)
        back[slot] = total.astype(BF16).reshape(8, 32, WIDTH)
        base = slots(7)
        copies = []
        for i in range(1, 8):
            h = lax.rem(head + i, 8)
            copies.append(
                send(base + i - 1, back.at[slot, h], columns(out, head), at_source(h))
            )
        own = pltpu.make_async_copy(back.at[slot, head], columns(out, head), own_sem.at[slot])
        own.start()
        return copies, own

    loads = [
        pltpu.make_async_copy(src, dst, load_sem.at[i])
        for i, (src, dst) in enumerate(
            (
                (w_gate_hbm.at[0], w_own.at[0]),
                (w_up_hbm.at[0], w_own.at[1]),
                (w_down_hbm.at[0], w_own.at[2]),
                (value_hbm, value_one),
                (rate_hbm, rate_turned),
                (step_hbm, step_ref),
                (columns(key_one, head), moved.at[0, core, head]),
                (columns(query_one, head), moved.at[2, core, head]),
                (columns(query_two, head), moved.at[3, core, head]),
            )
        )
    ]
    for load in loads:
        load.start()

    barrier = pltpu.get_barrier_semaphore()
    peers = [far(2), far(1), far(3)]
    peers += [(row, tok_z(i)) for i in (2, -2, 1, -1)] + [across, sibling]
    peers += [at_source(lax.rem(head + i, 8)) for i in range(1, 8)]
    for peer in peers:
        pl.semaphore_signal(barrier, inc=1, device_id=peer, device_id_type=MESH)

    @pl.when(other)
    def _():
        pl.semaphore_signal(barrier, inc=1, device_id=far(0), device_id_type=MESH)

    for load in loads[:3]:
        load.wait()
    shard[0] = w_own[...].astype(BF16)
    pl.semaphore_wait(barrier, len(peers) + jnp.where(same, 0, 1))

    gather_start(0)
    keys_in = spread(key_one, 0)
    for load in loads[3:]:
        load.wait()
    rates = rate_turned[...].astype(F32).T
    for h in range(8):
        block = pl.ds(h * WIDTH, WIDTH)
        product = rates[:, h : h + 1] * value_one[:, block].astype(F32)
        negated[:, block] = (-product).astype(BF16)
    targets_in = spread(negated, 1)
    moved[1, core, head] = negated[:, pl.ds(pl.multiple_of(head * WIDTH, WIDTH), WIDTH)]
    gather_two(0)
    keys_shared = share(keys_in, 0)
    targets_shared = share(targets_in, 1)
    gather_three(0)
    arrive(keys_shared)
    arrive(targets_shared)

    def gradients(chosen):
        keys, targets = moved[0].reshape(512, WIDTH), moved[1].reshape(512, WIDTH)
        gate, up, down = (matrix(0, chosen, i) for i in range(3))
        key_gate = dot_nt(gate, keys)
        key_up = dot_nt(up, keys)
        back_prod = dot_nt(down, targets)
        sig = jax.nn.sigmoid(key_gate)
        act = key_gate * sig
        hidden = (act * key_up).astype(BF16)
        gate_pre = (back_prod * key_up * sig * (1.0 + key_gate * (1.0 - sig))).astype(BF16)
        up_pre = (back_prod * act).astype(BF16)
        for which, (left, right) in enumerate(
            ((gate_pre, keys), (up_pre, keys), (hidden, targets))
        ):
            total = dot_nn(left, right).astype(BF16)
            for i, u in enumerate(chosen):
                sums[u, :, which] = total[64 * i : 64 * i + 64].reshape(4, 16, WIDTH)

    one_base, two_base, far_base = slots(12), slots(12), slots(4)
    wide, thin = {}, {}

    def send_wide(u):
        base = one_base + u * 3
        if u < 2:
            there = sums.at[u, pl.ds((1 - upper) * 2, 2)]
            wide[u] = [send(base, there, wide_in.at[u, pl.ds(0, 2)], across)]
        else:
            wide[u] = [
                send(
                    base + d - 1, sums.at[u, lax.rem(low + d, 4)], wide_in.at[u, d - 1], near(d, u)
                )
                for d in (1, 3, 2)
            ]

    def send_thin(u):
        arrive(wide[u])
        base = two_base + u * 3
        if u < 2:
            for i in range(2):
                total = sums[u, upper * 2 + i].astype(F32) + wide_in[u, i].astype(F32)
                narrow[u, 2 * i] = total[:, 0:8].astype(BF16)
                narrow[u, 2 * i + 1] = total[:, 8:16].astype(BF16)
            thin[u] = [
                send(
                    base + d - 1,
                    narrow.at[u, lax.rem(low + d, 4)],
                    narrow_in.at[u, d - 1],
                    near(d, u),
                )
                for d in (1, 3, 2)
            ]
        else:
            total = sums[u, low].astype(F32)
            for d in range(3):
                total += wide_in[u, d].astype(F32)
            narrow[u, 0] = total[:, 0:8].astype(BF16)
            narrow[u, 1] = total[:, 8:16].astype(BF16)
            thin[u] = [send(base, narrow.at[u, 1 - upper], narrow_in.at[u, 0], across)]

    def copy_last(u, j):
        return remote(far_base + j, last.at[u], last_in.at[j], far(j))

    def send_last(u):
        arrive(thin[u])
        if u < 2:
            total = narrow[u, low].astype(F32)
            for d in range(3):
                total += narrow_in[u, d].astype(F32)
        else:
            total = narrow[u, upper].astype(F32) + narrow_in[u, 0].astype(F32)
        last[u] = total.astype(BF16)
        j = lax.rem(u + 4 - high, 4)
        home = (j == 0) & same

        @pl.when(home)
        def _():
            last_in[0] = total.astype(BF16)

        @pl.when(jnp.logical_not(home))
        def _():
            copy_last(u, j).start()

    for chosen in PAIRS:
        for u in chosen:
            gathered(0, u)
        gradients(chosen)
        for u in chosen:
            send_wide(u)
    for u in PAIRS[0]:
        send_thin(u)
    for u in PAIRS[0]:
        send_last(u)
    for u in PAIRS[1]:
        send_thin(u)
    for u in PAIRS[1]:
        send_last(u)

    query_one_in = spread(query_one, 2)
    query_two_in = spread(query_two, 3)

    @pl.when(other)
    def _():
        copy_last(high, 0).wait_recv()

    total = last_in[0].astype(F32)
    for j in (1, 3, 2):
        copy_last(lax.rem(high + j, 4), j).wait_recv()
        total += last_in[j].astype(F32)

    step = step_ref[0]
    keep = []
    for which, new in enumerate((gate_new, up_new, down_new)):
        grads = total[which]
        scale = jnp.sqrt(jnp.mean(grads * grads, axis=1, keepdims=True) + 1e-06)
        renewed = w_own[which] - step * grads / scale
        fresh[which] = renewed
        keep.append(pltpu.make_async_copy(fresh.at[which], new.at[0], own_sem.at[which + 2]))
        keep[-1].start()
        shard[1, which] = renewed.astype(BF16)

    gather_start(1)
    one_shared = share(query_one_in, 2)
    two_shared = share(query_two_in, 3)
    arrive(one_shared)
    one_out, one_own = apply(2, 0, 0, out_one)
    gather_two(1)
    gather_three(1)
    arrive(two_shared)
    for u in range(4):
        gathered(1, u)
    two_out, two_own = apply(3, 1, 1, out_two)
    for copy in [one_own] + keep + [two_own]:
        copy.wait()
    arrive(one_out)
    for j in (1, 2, 3):
        copy_last(lax.rem(high + j, 4), j).wait_send()

    @pl.when(other)
    def _():
        copy_last(high, 0).wait_send()

    gather_end(0)
    gather_end(1)
    arrive(two_out)
    for copy in ends:
        copy.wait_send()


def write_out(*refs):
    sources, targets, held = refs[:5], refs[5:10], refs[10:15]
    sems = refs[15]
    into = [pltpu.make_async_copy(sources[i], held[i], sems.at[0, i]) for i in range(5)]
    out = [pltpu.make_async_copy(held[i], targets[i], sems.at[1, i]) for i in range(5)]
    for copy in into:
        copy.start()
    for i in range(5):
        into[i].wait()
        out[i].start()
    for copy in out:
        copy.wait()


def local(query_one, key_one, value_one, rate_one, query_two, w_gate, w_up, w_down, step_size):
    hbm = pl.BlockSpec(memory_space=pltpu.HBM)
    results = (
        jax.ShapeDtypeStruct(query_one.shape, BF16),
        jax.ShapeDtypeStruct(query_one.shape, BF16),
        jax.ShapeDtypeStruct(w_gate.shape, F32),
        jax.ShapeDtypeStruct(w_gate.shape, F32),
        jax.ShapeDtypeStruct(w_gate.shape, F32),
    )
    made = pl.pallas_call(
        kernel,
        out_shape=results,
        in_specs=[hbm] * 9,
        out_specs=(hbm,) * 5,
        scratch_shapes=[
            pltpu.SMEM((1,), F32),
            pltpu.VMEM((8, 32), BF16),
            pltpu.VMEM((32, 8 * WIDTH), BF16),
            pltpu.VMEM((3, 8, WIDTH), F32),
            pltpu.VMEM((3, 8, WIDTH), F32),
            pltpu.VMEM((2, 3, 8, WIDTH), BF16),
            pltpu.VMEM((2, 4, 3, 8, WIDTH), BF16),
            pltpu.VMEM((2, 4, 3, 3, 8, WIDTH), BF16),
            pltpu.VMEM((2, 4, 4, 3, 16, WIDTH), BF16),
            pltpu.VMEM((4, 2, 8, 32, WIDTH), BF16),
            pltpu.VMEM((32, 8 * WIDTH), BF16),
            pltpu.VMEM((2, 8, 32, WIDTH), BF16),
            pltpu.VMEM((2, 8, 32, WIDTH), BF16),
            pltpu.VMEM((2, 8, 32, WIDTH), BF16),
            pltpu.VMEM((4, 4, 3, 16, WIDTH), BF16),
            pltpu.VMEM((4, 3, 3, 16, WIDTH), BF16),
            pltpu.VMEM((4, 4, 3, 8, WIDTH), BF16),
            pltpu.VMEM((4, 3, 3, 8, WIDTH), BF16),
            pltpu.VMEM((4, 3, 8, WIDTH), BF16),
            pltpu.VMEM((4, 3, 8, WIDTH), BF16),
            pltpu.SemaphoreType.DMA((COPIES,)),
            pltpu.SemaphoreType.DMA((COPIES,)),
            pltpu.SemaphoreType.DMA((9,)),
            pltpu.SemaphoreType.DMA((5,)),
        ],
        compiler_params=pltpu.CompilerParams(
            collective_id=0, has_side_effects=True, vmem_limit_bytes=62 * 1024 * 1024
        ),
        cost_estimate=pl.CostEstimate(
            flops=1700000000, bytes_accessed=2000000, transcendentals=400000
        ),
    )(step_size, rate_one.T, query_one, key_one, value_one, query_two, w_gate, w_up, w_down)
    return pl.pallas_call(
        write_out,
        out_shape=results,
        in_specs=[hbm] * 5,
        out_specs=(hbm,) * 5,
        scratch_shapes=[pltpu.VMEM(made[i].shape, made[i].dtype) for i in range(5)]
        + [pltpu.SemaphoreType.DMA((2, 5))],
        compiler_params=pltpu.CompilerParams(vmem_limit_bytes=62 * 1024 * 1024),
    )(*made)


def solution(mesh):
    rows = P(("head", "tok"), None)
    shards = P("head", "tok", None)
    return jax.shard_map(
        local,
        mesh=mesh,
        in_specs=(rows,) * 5 + (shards,) * 3 + (P("head"),),
        out_specs=(rows,) * 2 + (shards,) * 3,
        check_vma=False,
    )
```

time: 96.8 us -> 90.2 us (0.932)
  Pallas kernels: 95.3 us -> 88.7 us
    pallas_call x1, Pallas kernels: 93.4 us -> 86.9 us  [local(): pl.pallas_call(kernel, out_shape=results, in_specs=[hbm] * 9, out_specs=(...]
where the time goes in v3:
time: 90.2 us; the launch traced here: 90 us
  Pallas kernels  88.7 us (98%)
  between operations  1.29 us (1%)
    pallas_call x1, Pallas kernels, local(): pl.pallas_call(kernel, out_shape=results, in_specs=[hbm] * 9, out_specs=(...  86.9 us
    pallas_call x1, Pallas kernels, local(): pl.pallas_call(write_out, out_shape=results, in_specs=[hbm] * 5, out_spec...  1.83 us

profile of v3, /device:TPU:1, one launch (start us, length us, event | category | flops | bytes accessed | tf_op | source)
XLA Modules:
  0.0 90.0 jit_solution(6901339378407808418)
XLA Ops:
  1.3 86.9 %shard_map.128 = (bf16[32,4096]{1,0:T(8,128)(2,1)}, bf16[32,4096]{1,0:T(8,128)(2,1)}, f32[1,8,512]{2,1,0:T(8,128)}, f32[1,8,512]{2,1,0:T(8,128)}, f32[1,8,512]{2,1,0:T(8,128)}) custom-call(f32[1]{0:T(128)S(6)} %copy.14.step_hbm, bf16[8,32]{1,0:T(8,128)(2,1)} %bitcast.1, bf16[32,4096]{1,0:T(8,128)(2,1)} %query_one.1, bf16[32,4096]{1,0:T(8,128)(2,1)} %key_one.1, ...), custom_call_target="tpu_custom_call" | custom-call | flops 1700000000 | bytes 2000000 | tf_op jit(solution)/shard_map/pallas_call | solution.py:495
  88.2 1.8 %shard_map.129 = (bf16[32,4096]{1,0:T(8,128)(2,1)}, bf16[32,4096]{1,0:T(8,128)(2,1)}, f32[1,8,512]{2,1,0:T(8,128)}, f32[1,8,512]{2,1,0:T(8,128)}, f32[1,8,512]{2,1,0:T(8,128)}) custom-call(bf16[32,4096]{1,0:T(8,128)(2,1)} %get-tuple-element.10.refs_0_, bf16[32,4096]{1,0:T(8,128)(2,1)} %get-tuple-element.11.refs_1_, f32[1,8,512]{2,1,0:T(8,128)} %get-tuple-element.12.refs_2_, ...), custom_call_target="tpu_custom_call" | custom-call | tf_op jit(solution)/shard_map/pallas_call | solution.py:533

commit v4 on v3

--- a/solution.py
+++ b/solution.py
@@ -318,6 +318,7 @@
     keys_shared = share(keys_in, 0)
     targets_shared = share(targets_in, 1)
     gather_three(0)
+    query_one_in = spread(query_one, 2)
     arrive(keys_shared)
     arrive(targets_shared)
 
@@ -411,15 +412,16 @@
             send_wide(u)
     for u in PAIRS[0]:
         send_thin(u)
+    for u in PAIRS[1]:
+        send_thin(u)
+    one_shared = share(query_one_in, 2)
     for u in PAIRS[0]:
         send_last(u)
     for u in PAIRS[1]:
-        send_thin(u)
-    for u in PAIRS[1]:
         send_last(u)
 
-    query_one_in = spread(query_one, 2)
-    query_two_in = spread(query_two, 3)
+    arrive(one_shared)
+    one_out, one_own = apply(2, 0, 0, out_one)
 
     @pl.when(other)
     def _():
@@ -442,12 +444,10 @@
         shard[1, which] = renewed.astype(BF16)
 
     gather_start(1)
-    one_shared = share(query_one_in, 2)
-    two_shared = share(query_two_in, 3)
-    arrive(one_shared)
-    one_out, one_own = apply(2, 0, 0, out_one)
+    query_two_in = spread(query_two, 3)
     gather_two(1)
     gather_three(1)
+    two_shared = share(query_two_in, 3)
     arrive(two_shared)
     for u in range(4):
         gathered(1, u)

time: 90.2 us -> 87.1 us (0.966)
  Pallas kernels: 88.7 us -> 85.6 us
    pallas_call x1, Pallas kernels: 86.9 us -> 83.8 us  [local(): pl.pallas_call(kernel, out_shape=results, in_specs=[hbm] * 9, out_specs=(...]
where the time goes in v4:
time: 87.1 us; the launch traced here: 86.9 us
  Pallas kernels  85.6 us (98%)
  between operations  1.29 us (1%)
    pallas_call x1, Pallas kernels, local(): pl.pallas_call(kernel, out_shape=results, in_specs=[hbm] * 9, out_specs=(...  83.8 us
    pallas_call x1, Pallas kernels, local(): pl.pallas_call(write_out, out_shape=results, in_specs=[hbm] * 5, out_spec...  1.83 us

profile of v4, /device:TPU:1, one launch (start us, length us, event | category | flops | bytes accessed | tf_op | source)
XLA Modules:
  0.0 86.9 jit_solution(12234863156198541872)
XLA Ops:
  1.3 83.8 %shard_map.128 = (bf16[32,4096]{1,0:T(8,128)(2,1)}, bf16[32,4096]{1,0:T(8,128)(2,1)}, f32[1,8,512]{2,1,0:T(8,128)}, f32[1,8,512]{2,1,0:T(8,128)}, f32[1,8,512]{2,1,0:T(8,128)}) custom-call(f32[1]{0:T(128)S(6)} %copy.14.step_hbm, bf16[8,32]{1,0:T(8,128)(2,1)} %bitcast.1, bf16[32,4096]{1,0:T(8,128)(2,1)} %query_one.1, bf16[32,4096]{1,0:T(8,128)(2,1)} %key_one.1, ...), custom_call_target="tpu_custom_call" | custom-call | flops 1700000000 | bytes 2000000 | tf_op jit(solution)/shard_map/pallas_call | solution.py:495
  85.1 1.8 %shard_map.129 = (bf16[32,4096]{1,0:T(8,128)(2,1)}, bf16[32,4096]{1,0:T(8,128)(2,1)}, f32[1,8,512]{2,1,0:T(8,128)}, f32[1,8,512]{2,1,0:T(8,128)}, f32[1,8,512]{2,1,0:T(8,128)}) custom-call(bf16[32,4096]{1,0:T(8,128)(2,1)} %get-tuple-element.10.refs_0_, bf16[32,4096]{1,0:T(8,128)(2,1)} %get-tuple-element.11.refs_1_, f32[1,8,512]{2,1,0:T(8,128)} %get-tuple-element.12.refs_2_, ...), custom_call_target="tpu_custom_call" | custom-call | tf_op jit(solution)/shard_map/pallas_call | solution.py:533

commit v5 on v4

--- a/solution.py
+++ b/solution.py
@@ -155,7 +155,7 @@
         if along_z:
             return [
                 remote(base + d - 1, block, near_in.at[g, u, d - 1], near(d, u))
-                for d in (1, 3, 2)
+                for d in (2, 1, 3)
             ]
         return [remote(base, block, near_in.at[g, u, 0], across)]
 
@@ -163,7 +163,7 @@
         base = bases[g][2] + u * 3
         if along_z:
             block = weights.at[g, u, low]
-            return [remote(base + d - 1, block, block, near(d, u)) for d in (1, 3, 2)]
+            return [remote(base + d - 1, block, block, near(d, u)) for d in (2, 1, 3)]
         block = weights.at[g, u, pl.ds(upper * 2, 2)]
         return [remote(base, block, block, across)]
 
@@ -315,9 +315,9 @@
     targets_in = spread(negated, 1)
     moved[1, core, head] = negated[:, pl.ds(pl.multiple_of(head * WIDTH, WIDTH), WIDTH)]
     gather_two(0)
+    gather_three(0)
     keys_shared = share(keys_in, 0)
     targets_shared = share(targets_in, 1)
-    gather_three(0)
     query_one_in = spread(query_one, 2)
     arrive(keys_shared)
     arrive(targets_shared)
@@ -353,7 +353,7 @@
                 send(
                     base + d - 1, sums.at[u, lax.rem(low + d, 4)], wide_in.at[u, d - 1], near(d, u)
                 )
-                for d in (1, 3, 2)
+                for d in (2, 1, 3)
             ]
 
     def send_thin(u):
@@ -371,7 +371,7 @@
                     narrow_in.at[u, d - 1],
                     near(d, u),
                 )
-                for d in (1, 3, 2)
+                for d in (2, 1, 3)
             ]
         else:
             total = sums[u, low].astype(F32)

time: 87.1 us -> 86.5 us (level)
  no operation moved by 1% of the time
where the time goes in v5:
time: 86.5 us; the launch traced here: 86.3 us
  Pallas kernels  85 us (98%)
  between operations  1.29 us (1%)
    pallas_call x1, Pallas kernels, local(): pl.pallas_call(kernel, out_shape=results, in_specs=[hbm] * 9, out_specs=(...  83.2 us
    pallas_call x1, Pallas kernels, local(): pl.pallas_call(write_out, out_shape=results, in_specs=[hbm] * 5, out_spec...  1.83 us

profile of v5, /device:TPU:1, one launch (start us, length us, event | category | flops | bytes accessed | tf_op | source)
XLA Modules:
  0.0 86.3 jit_solution(3667580341221996387)
XLA Ops:
  1.3 83.2 %shard_map.128 = (bf16[32,4096]{1,0:T(8,128)(2,1)}, bf16[32,4096]{1,0:T(8,128)(2,1)}, f32[1,8,512]{2,1,0:T(8,128)}, f32[1,8,512]{2,1,0:T(8,128)}, f32[1,8,512]{2,1,0:T(8,128)}) custom-call(f32[1]{0:T(128)S(6)} %copy.14.step_hbm, bf16[8,32]{1,0:T(8,128)(2,1)} %bitcast.1, bf16[32,4096]{1,0:T(8,128)(2,1)} %query_one.1, bf16[32,4096]{1,0:T(8,128)(2,1)} %key_one.1, ...), custom_call_target="tpu_custom_call" | custom-call | flops 1700000000 | bytes 2000000 | tf_op jit(solution)/shard_map/pallas_call | solution.py:495
  84.5 1.8 %shard_map.129 = (bf16[32,4096]{1,0:T(8,128)(2,1)}, bf16[32,4096]{1,0:T(8,128)(2,1)}, f32[1,8,512]{2,1,0:T(8,128)}, f32[1,8,512]{2,1,0:T(8,128)}, f32[1,8,512]{2,1,0:T(8,128)}) custom-call(bf16[32,4096]{1,0:T(8,128)(2,1)} %get-tuple-element.10.refs_0_, bf16[32,4096]{1,0:T(8,128)(2,1)} %get-tuple-element.11.refs_1_, f32[1,8,512]{2,1,0:T(8,128)} %get-tuple-element.12.refs_2_, ...), custom_call_target="tpu_custom_call" | custom-call | tf_op jit(solution)/shard_map/pallas_call | solution.py:533
